TPU v7x, 32 devices: a whole 2x2x4 slice. The times are simulated.
32 devices in a mesh: rows: 8 (over z, x), modes: 4 (over y, core).
Axes of the slice: x: 2, y: 2, z: 4, core: 2. Of those that a mesh axis runs over, the one named last changes fastest.
Arguments:
- snapshots: bfloat16 [1024, 5, 6144], P(None, None, 'rows')
- eigvec: bfloat16 [1024, 256], P('rows', 'modes'), may hold values from -0.1875 to 0.1875
- eigval: float32 [256], replicated, may hold values from 30720 to 245760
- jac_self: bfloat16 [5, 5, 6144], P(None, None, 'rows'), may hold values from -0.5 to 1.5
- jac_off: bfloat16 [6, 5, 5, 6144], P(None, None, None, 'rows'), may hold values from -1 to 1
- neighbor: int32 [6, 6144], P(None, 'rows'), may hold values from 0 to 1279
- send_list: int32 [2, 2048], P(None, 'rows'), may hold values from 0 to 767
- send_count: int32 [2, 8], P(None, 'rows'), may hold values from 1 to 256
- owned_cells: int32 [8], P('rows'), may hold values from 1 to 768, 4608 in all
Outputs:
- test_basis: bfloat16 [256, 5, 6144], P('modes', None, 'rows')
- reduced: float32 [256, 256], P('rows', 'modes')
Inputs may be any that keep to these rules, and one draw needn't show every extreme that they name: neighbor[b, c] indexes the extended slots of the cell's own partition: its 768 own slots, then 256 lower ghost slots, then 256 upper ghost slots. `send_list`: entries of partition p's lists are local slots of partition p.
All inputs are finite; a program needn't handle non-finite values. No bound on the sum of `owned_cells` on one device may be relied on, other than what follows from the above.
Results may differ from a plain program's by a relative error of at most 0.0049.
Values may be sent and summed in bfloat16 or wider, within the bound.
A program may use at most 128 MiB of HBM per device.

v0:
```python
import jax
import jax.numpy as jnp
from jax import lax
from jax.sharding import PartitionSpec as P


def passed_along(value, axis, steps):
    count = lax.axis_size(axis)
    first, last = (max(0, -steps), min(count, count - steps))
    return lax.ppermute(value, axis, [(source, source + steps) for source in range(first, last)])


def neighbour_rows(piece, offset):
    return passed_along(piece, "rows", offset)


def shards(
    snapshots, eigvec, eigval, jac_self, jac_off, neighbor, send_list, send_count, owned_cells
):
    snap_count, var_count, cell_count = snapshots.shape
    panel_width = eigvec.shape[1]
    halo_slots = send_list.shape[1]
    snap_rows = snapshots.reshape(snap_count, var_count * cell_count)
    modes_sum = lax.dot_general(
        lax.all_gather(eigvec, "rows", axis=0, tiled=True),
        snap_rows,
        (((0,), (0,)), ((), ())),
        preferred_element_type=jnp.float32,
    )
    owned_mask = jnp.arange(cell_count, dtype=jnp.int32)[None, None, :] < owned_cells[0]
    modes = jnp.where(
        owned_mask,
        modes_sum.reshape(panel_width, var_count, cell_count),
        jnp.zeros((), jnp.float32),
    ).astype(jnp.bfloat16)
    picked = jnp.take(modes, send_list.reshape(-1), axis=2).reshape(
        panel_width, var_count, 2, halo_slots
    )
    live_slots = jnp.arange(halo_slots, dtype=jnp.int32)[None, :] < send_count
    picked = jnp.where(live_slots[None, None], picked, jnp.zeros((), jnp.bfloat16))
    from_below = neighbour_rows(picked[:, :, 1], 1)
    from_above = neighbour_rows(picked[:, :, 0], -1)
    extended = jnp.concatenate([modes, from_below, from_above], axis=2)
    own_term = jnp.einsum("vwc,mwc->mvc", jac_self, modes, preferred_element_type=jnp.float32)
    neighbours = jnp.take(extended, neighbor, axis=2)
    off_term = jnp.einsum("bvwc,mwbc->mvc", jac_off, neighbours, preferred_element_type=jnp.float32)
    test_local = jnp.where(owned_mask, own_term + off_term, jnp.zeros((), jnp.float32)).astype(
        jnp.bfloat16
    )
    products = lax.dot_general(
        snap_rows,
        test_local.reshape(panel_width, var_count * cell_count),
        (((1,), (1,)), ((), ())),
        preferred_element_type=jnp.float32,
    )
    shares = lax.psum_scatter(products, "rows", scatter_dimension=0, tiled=True)
    eigvec_rows = lax.all_gather(eigvec, "modes", axis=1, tiled=True)
    partial_sum = jnp.dot(
        eigvec_rows.astype(jnp.float32).T, shares, precision=lax.Precision.HIGHEST
    )
    reduced_part = lax.psum_scatter(partial_sum, "rows", scatter_dimension=0, tiled=True)
    rows_out = reduced_part.shape[0]
    scales = 1.0 / jnp.sqrt(eigval)
    row_scales = lax.dynamic_slice_in_dim(scales, lax.axis_index("rows") * rows_out, rows_out, 0)
    col_scales = lax.dynamic_slice_in_dim(
        scales, lax.axis_index("modes") * panel_width, panel_width, 0
    )
    reduced = reduced_part * row_scales[:, None] * col_scales[None, :]
    return (test_local, reduced)


def solution(mesh):
    in_specs = (
        P(None, None, "rows"),
        P("rows", "modes"),
        P(),
        P(None, None, "rows"),
        P(None, None, None, "rows"),
        P(None, "rows"),
        P(None, "rows"),
        P(None, "rows"),
        P("rows"),
    )
    out_specs = (P("modes", None, "rows"), P("rows", "modes"))
    return jax.shard_map(shards, mesh=mesh, in_specs=in_specs, out_specs=out_specs, check_vma=False)
```

profile of v0, /device:TPU:0, one launch (start us, length us, event | category | flops | bytes accessed | tf_op | source)
XLA Modules:
  0.0 272.5 jit_solution(6265888050190093898)
XLA Ops:
  7.9 10.7 %copy.30 = bf16[1024,5,768]{0,2,1:T(8,128)(2,1)} copy(bf16[1024,5,768]{2,0,1:T(8,128)(2,1)} %param.9) | data formatting | bytes 15728640 | tf_op args[0]
  18.6 27.9 %all_gather.6 = bf16[1024,64]{0,1:T(8,128)(2,1)S(1)} all-gather(bf16[128,64]{0,1:T(8,128)(2,1)S(1)} %copy-done.3), channel_id=1, replica_groups=mesh['rows'=8,'modes'=4] {'rows'}, dimensions={0}, use_global_device_ids=true | all-gather | bytes 147456 | tf_op jit(solution)/shard_map/all_gather | solution.py:25
  46.5 5.7 %fusion.8 = bf16[64,5,768]{2,0,1:T(8,128)(2,1)S(1)} fusion(bf16[1024,5,768]{0,2,1:T(8,128)(2,1)} %copy.30, pred[768]{0:T(1024)(128)(4,1)S(1)} %iota_compare_fusion, bf16[1024,64]{0,1:T(8,128)(2,1)S(1)} %all_gather.6), kind=kOutput, calls=%fused_computation.10 | convolution fusion | flops 503808000 | bytes 8487680 | tf_op jit(solution)/shard_map/dot_general | solution.py:24
  52.2 1.1 copy.31
  53.4 1.8 gather_fusion
  55.8 3.4 %collective-permute-start = (bf16[64,5,256]{2,0,1:T(8,128)(2,1)S(1)}, bf16[64,5,256]{2,0,1:T(8,128)(2,1)S(1)}, u32[]{:S(2)}, u32[]{:S(2)}) collective-permute-start(bf16[64,5,256]{2,0,1:T(8,128)(2,1)S(1)} %get-tuple-element.8), channel_id=1, source_target_pairs={{0,4},{4,8},{8,12},{12,16},{16,20},{20,24},{24,28},{1,5},{5,9},{9,... | collective-permute-start | bytes 491528 | tf_op jit(solution)/shard_map/ppermute | solution.py:10
  59.2 1.5 collective-permute-start.1
  60.8 6.7 %copy.39 = bf16[6,5,5,768]{0,1,2,3:T(8,128)(2,1)} copy(bf16[6,5,5,768]{3,0,2,1:T(8,128)(2,1)} %param.13) | data formatting | bytes 460800 | tf_op args[4]
  67.5 1.9 copy.32
  69.4 1.0 pad_maximum_fusion
  70.4 2.9 %copy.36 = bf16[64,5,1280]{0,1,2:T(8,128)(2,1)S(1)} copy(bf16[64,5,1280]{2,0,1:T(8,128)(2,1)S(1)} %pad_maximum_fusion) | data formatting | bytes 1638400 | tf_op jit(solution)/shard_map/concatenate | solution.py:43
  73.3 12.9 %gather_fusion.1 = bf16[4608,64,5]{1,2,0:T(8,128)(2,1)} fusion(bf16[64,5,1280]{0,1,2:T(8,128)(2,1)S(1)} %copy.36, s32[5120]{0:T(1024)S(1)} %pad_clamp_fusion), kind=kCustom, calls=%fused_computation.1 | custom fusion | bytes 5916672 | tf_op jit(solution)/shard_map/jit(_take)/gather | solution.py:45
  86.2 9.9 %copy.46 = bf16[6,768,64,5]{1,0,2,3:T(8,128)(2,1)} copy(bf16[6,768,64,5]{2,3,1,0:T(8,128)(2,1)} %bitcast.58) | data formatting | bytes 5898240 | tf_op jit(solution)/shard_map/jit(_take)/gather | solution.py:45
  96.1 4.5 %select_bitcast_fusion = bf16[64,5,6,768]{3,2,0,1:T(8,128)(2,1)} fusion(bf16[6,768,64,5]{1,0,2,3:T(8,128)(2,1)} %copy.46, pred[6,768]{1,0:T(8,128)(4,1)S(1)} %compare_and_fusion), kind=kLoop, calls=%fused_computation.4 | loop fusion | flops 1474560 | bytes 5902848 | tf_op jit(solution)/shard_map/jit(_take)/select_n | solution.py:45
  100.5 14.5 %copy.38 = bf16[64,5,6,768]{0,2,1,3:T(8,128)(2,1)} copy(bf16[64,5,6,768]{3,2,0,1:T(8,128)(2,1)} %select_bitcast_fusion) | data formatting | bytes 5898240 | tf_op jit(solution)/shard_map/jit(_take)/select_n | solution.py:45
  115.0 9.6 %fusion.12 = f32[768,64,5,1]{1,2,3,0:T(8,128)S(1)} fusion(bf16[64,5,6,768]{0,2,1,3:T(8,128)(2,1)} %copy.38, bf16[6,5,5,768]{0,1,2,3:T(8,128)(2,1)} %copy.39), kind=kOutput, calls=%fused_computation.28 | convolution fusion | flops 14745600 | bytes 4162560 | tf_op jit(solution)/shard_map/bvwc,mwbc->mvc/dot_general | solution.py:46
  124.7 5.0 %fusion.4 = bf16[64,5,768]{0,1,2:T(8,128)(2,1)} fusion(f32[768,64,5,1]{1,2,3,0:T(8,128)S(1)} %fusion.12, bf16[64,5,768]{0,1,2:T(8,128)(2,1)} %copy-done, bf16[5,5,768]{1,0,2:T(8,128)(2,1)} %copy.32, pred[768]{0:T(1024)(128)(4,1)S(1)} %iota_compare_fusion), kind=kOutput, calls=%fused_computation.8 | convolution fusion | flops 3194880 | bytes 2005248 | tf_op jit(solution)/shard_map/vwc,mwc->mvc/dot_general | solution.py:44
  129.7 1.8 copy.41
  131.5 6.6 %convolution_bitcast_fusion = f32[1024,64]{0,1:T(8,128)} fusion(bf16[64,5,768]{2,0,1:T(8,128)(2,1)S(1)} %copy.41, bf16[1024,5,768]{2,0,1:T(8,128)(2,1)} %param.9), kind=kOutput, calls=%fused_computation.11 | convolution fusion | flops 503316480 | bytes 8617984 | tf_op jit(solution)/shard_map/dot_general | solution.py:50
  138.2 5.2 %all_gather.7 = bf16[128,256]{0,1:T(8,128)(2,1)S(1)} all-gather(bf16[128,64]{0,1:T(8,128)(2,1)S(1)} %copy-done.3), channel_id=1, replica_groups=mesh['rows'=8,'modes'=4] {'modes'}, dimensions={1}, use_global_device_ids=true | all-gather | bytes 81920 | tf_op jit(solution)/shard_map/all_gather | solution.py:57
  143.4 57.5 %reduce-scatter.5.cloned.1.call-done = f32[128,64]{0,1:T(8,128)} async-done(((f32[1024,64]{0,1:T(8,128)}), f32[128,64]{0,1:T(8,128)}) %reduce-scatter.5.cloned.1.call-update) | async-done | bytes 32784 | tf_op jit(solution)/shard_map/reduce_scatter | solution.py:56
  200.9 1.0 convolution_bitcast_fusion.1
  202.8 61.3 %reduce-scatter.7.cloned.1.call-done = f32[32,64]{1,0:T(8,128)} async-done(((f32[256,64]{1,0:T(8,128)}), f32[32,64]{1,0:T(8,128)}) %reduce-scatter.7.cloned.1.call-update) | async-done | bytes 8208
  264.1 0.8 copy.48
  (40 shorter events, 2.5 us)
Async XLA Ops:
  7.2 193.7 %reduce-scatter.5.cloned.1.call-start = ((), (), s32[]{:S(2)}) async-start(), calls=%async_computation.2 | async-start | bytes 294912 | tf_op jit(solution)/shard_map/reduce_scatter | solution.py:56
  7.9 10.7 %copy-start.3 = (bf16[128,64]{0,1:T(8,128)(2,1)S(1)}, bf16[128,64]{0,1:T(8,128)(2,1)}, u32[]{:S(2)}) copy-start(bf16[128,64]{0,1:T(8,128)(2,1)} %param.10) | copy-start | bytes 49156
  46.5 6.9 %copy-start.5 = (s32[2,256]{1,0:T(2,128)S(1)}, s32[2,256]{1,0:T(2,128)}, u32[]{:S(2)}) copy-start(s32[2,256]{1,0:T(2,128)} %param.15) | copy-start | bytes 6148
  52.2 3.5 %copy-start.7 = (s32[2,1]{0,1:T(1,128)S(1)}, s32[2,1]{0,1:T(1,128)}, u32[]{:S(2)}) copy-start(s32[2,1]{0,1:T(1,128)} %param.16) | copy-start | bytes 28
  52.2 8.5 %copy-start.2 = (s32[6,768]{1,0:T(8,128)S(1)}, s32[6,768]{1,0:T(8,128)}, u32[]{:S(2)}) copy-start(s32[6,768]{1,0:T(8,128)} %param.14) | copy-start | bytes 55300
  53.3 14.2 %copy-start = (bf16[64,5,768]{0,1,2:T(8,128)(2,1)}, bf16[64,5,768]{0,1,2:T(8,128)(2,1)S(1)}, u32[]{:S(2)}) copy-start(bf16[64,5,768]{0,1,2:T(8,128)(2,1)S(1)} %copy.31) | copy-start | bytes 1474564
  55.8 13.6 %collective-permute-start = (bf16[64,5,256]{2,0,1:T(8,128)(2,1)S(1)}, bf16[64,5,256]{2,0,1:T(8,128)(2,1)S(1)}, u32[]{:S(2)}, u32[]{:S(2)}) collective-permute-start(bf16[64,5,256]{2,0,1:T(8,128)(2,1)S(1)} %get-tuple-element.8), channel_id=1, source_target_pairs={{0,4},{4,8},{8,12},{12,16},{16,20},{20,24},{24,28},{1,5},{5,9},{9,... | collective-permute-start | bytes 491528 | tf_op jit(solution)/shard_map/ppermute | solution.py:10
  59.2 10.2 %collective-permute-start.1 = (bf16[64,5,256]{2,0,1:T(8,128)(2,1)S(1)}, bf16[64,5,256]{2,0,1:T(8,128)(2,1)}, u32[]{:S(2)}, u32[]{:S(2)}) collective-permute-start(bf16[64,5,256]{2,0,1:T(8,128)(2,1)S(1)} %get-tuple-element.9), channel_id=1, source_target_pairs={{4,0},{8,4},{12,8},{16,12},{20,16},{24,20},{28,24},{5,1},{9,5},{13... | collective-permute-start | bytes 491528 | tf_op jit(solution)/shard_map/ppermute | solution.py:10
  60.8 6.7 %copy-start.4 = (bf16[5,5,768]{2,1,0:T(8,128)(2,1)S(1)}, bf16[5,5,768]{2,1,0:T(8,128)(2,1)}, u32[]{:S(2)}) copy-start(bf16[5,5,768]{2,1,0:T(8,128)(2,1)} %param.12) | copy-start | bytes 115204
  131.5 6.6 %copy-start.1 = (bf16[64,5,768]{2,0,1:T(8,128)(2,1)}, bf16[64,5,768]{2,0,1:T(8,128)(2,1)S(1)}, u32[]{:S(2)}) copy-start(bf16[64,5,768]{2,0,1:T(8,128)(2,1)S(1)} %copy.41) | copy-start | bytes 1474564
  131.5 71.2 %copy-start.6 = (f32[256]{0:T(256)S(1)}, f32[256]{0:T(256)}, u32[]{:S(2)}) copy-start(f32[256]{0:T(256)} %param.11) | copy-start | bytes 3076
  138.1 126.0 %reduce-scatter.7.cloned.1.call-start = ((), (), s32[]{:S(2)}) async-start(), calls=%async_computation.3 | async-start | bytes 147456
Sparse Core Ops, SparseCore 0:
  138.2 62.6 reduce-scatter.4
  204.2 59.8 reduce-scatter.6
where the time goes:
time: 274 us; the launch traced here: 273 us
  waiting for transfers between devices  119 us (43%)
  local copies, waits for them, and re-layouts  67.1 us (24%)
  blocking collectives  33.1 us (12%)
  matrix products  27.9 us (10%)
  between operations  14.9 us (5%)
  other arithmetic  5.69 us (2%)
  starting transfers between devices  4.97 us (2%)
    unnamed x3, waiting for transfers between devices  61.3 us
    reduce_scatter x1, waiting for transfers between devices, shards(): shares = lax.psum_scatter(products, 'rows', scatter_dimension=0, tiled=True)  57.5 us
    all_gather x1, blocking collectives, shards(): lax.all_gather(eigvec, 'rows', axis=0, tiled=True)  27.9 us
    unnamed x24, local copies, waits for them, and re-layouts  23.4 us
    gather x2, local copies, waits for them, and re-layouts, shards(): neighbours = jnp.take(extended, neighbor, axis=2)  22.8 us
    select_n x1, local copies, waits for them, and re-layouts, shards(): neighbours = jnp.take(extended, neighbor, axis=2)  14.5 us
    dot_general x1, matrix products, shards(): jnp.einsum('bvwc,mwbc->mvc', jac_off, neighbours, preferred_element_type=...  9.62 us
    dot_general x1, matrix products, shards(): lax.dot_general(snap_rows, test_local.reshape(panel_width, var_count * ce...  6.58 us
  transfers between devices with their start and end apart: 4, of which 2 were waited for; matrix products, arithmetic and copies ran while one was open for 3% of the time, Pallas kernels for 0%

commit v1 on v0

v1 whole, which is shorter than its diff:
```python
import functools

import jax
import jax.numpy as jnp
from jax import lax
from jax.experimental import pallas as pl
from jax.experimental.pallas import tpu as pltpu
from jax.sharding import PartitionSpec as P

MESH = pl.DeviceIdType.MESH
F32 = jnp.float32
BF16 = jnp.bfloat16


def one_hot(index_row, start, depth):
    rows = lax.broadcasted_iota(jnp.int32, (depth, index_row.shape[1]), 0) + start
    return jnp.where(rows == index_row, 1.0, 0.0).astype(BF16)


def kernel(
    count_rows, count_modes,
    snap_hbm, ev_ref, eigval_ref, jself_ref, joff_ref, nbr_ref, slist_ref, scount_ref, owned_ref,
    test_ref, red_ref,
    snap, full, ext, pack, hot_send, hot_own, hot_ghost, near, acc, prod, out_box, in_box,
    snap_sem, ev_send, ev_recv, fan_send, fan_recv, halo_send, halo_recv, red_send, red_recv,
):
    p = lax.axis_index("rows")
    j = lax.axis_index("modes")
    var_count, snap_count, cells = snap.shape
    panel, depth = ev_ref.shape
    off_count = nbr_ref.shape[0]
    halo = slist_ref.shape[1]
    rows_out = red_ref.shape[0]
    half = rows_out // 2

    snap_copies = [
        pltpu.make_async_copy(snap_hbm.at[v], snap.at[v], snap_sem.at[v]) for v in range(var_count)
    ]
    for copy in snap_copies:
        copy.start()

    def row_peer(k):
        return lax.rem(p + k, count_rows)

    def mode_peer(k):
        return lax.rem(j + k, count_modes)

    barrier = pltpu.get_barrier_semaphore()
    for k in range(1, count_rows):
        pl.semaphore_signal(barrier, inc=1, device_id=(row_peer(k), j), device_id_type=MESH)
    for k in range(1, count_modes):
        pl.semaphore_signal(barrier, inc=1, device_id=(p, mode_peer(k)), device_id_type=MESH)
    pl.semaphore_wait(barrier, count_rows + count_modes - 2)

    def panel_slice(panel_index, source):
        return full.at[
            pl.ds(pl.multiple_of(panel_index * panel, panel), panel),
            pl.ds(pl.multiple_of(source * depth, depth), depth),
        ]

    def ev_copy(k, source):
        return pltpu.make_async_remote_copy(
            src_ref=ev_ref, dst_ref=panel_slice(j, source), send_sem=ev_send.at[k - 1],
            recv_sem=ev_recv.at[k - 1], device_id=(row_peer(k), j), device_id_type=MESH,
        )

    for k in range(1, count_rows):
        ev_copy(k, p).start()

    full[
        pl.ds(pl.multiple_of(j * panel, panel), panel), pl.ds(pl.multiple_of(p * depth, depth), depth)
    ] = ev_ref[...]

    slot = lax.broadcasted_iota(jnp.int32, (1, halo), 1)
    for way in range(2):
        picks = jnp.where(slot < scount_ref[way, 0], slist_ref[pl.ds(way, 1), :], -1)
        hot_send[:, way * halo:(way + 1) * halo] = one_hot(picks, 0, cells)

    @pl.loop(0, off_count)
    def _(b):
        picks = nbr_ref[pl.ds(b, 1), :]
        hot_own[b] = one_hot(picks, 0, cells)
        hot_ghost[b] = one_hot(picks, cells, 2 * halo)

    @pl.when(p == 0)
    def _():
        ext[:, cells:cells + halo] = jnp.zeros((var_count * panel, halo), BF16)

    @pl.when(p == count_rows - 1)
    def _():
        ext[:, cells + halo:] = jnp.zeros((var_count * panel, halo), BF16)

    for k in range(1, count_rows):
        ev_copy(k, lax.rem(p + count_rows - k, count_rows)).wait_recv()

    def fan_copy(k, panel_index):
        piece = full.at[pl.ds(pl.multiple_of(panel_index * panel, panel), panel), :]
        return pltpu.make_async_remote_copy(
            src_ref=piece, dst_ref=piece, send_sem=fan_send.at[k - 1], recv_sem=fan_recv.at[k - 1],
            device_id=(p, mode_peer(k)), device_id_type=MESH,
        )

    for k in range(1, count_modes):
        fan_copy(k, j).start()

    live = lax.broadcasted_iota(jnp.int32, (1, cells), 1) < owned_ref[0]

    def halo_copy(v, way):
        start = cells + (1 - way) * halo
        target = p + 1 if way else p - 1
        return pltpu.make_async_remote_copy(
            src_ref=pack.at[way, pl.ds(v * panel, panel), :],
            dst_ref=ext.at[pl.ds(v * panel, panel), pl.ds(start, halo)],
            send_sem=halo_send.at[way, v], recv_sem=halo_recv.at[way, v],
            device_id=(target, j), device_id_type=MESH,
        )

    mine = full[pl.ds(pl.multiple_of(j * panel, panel), panel), :]
    for v in range(var_count):
        snap_copies[v].wait()
        own = jnp.dot(mine, snap[v], preferred_element_type=F32)
        own = jnp.where(live, own, 0.0).astype(BF16)
        ext[v * panel:(v + 1) * panel, :cells] = own
        sent = jnp.dot(own, hot_send[...], preferred_element_type=F32).astype(BF16)
        for way in range(2):
            pack[way, v * panel:(v + 1) * panel, :] = sent[:, way * halo:(way + 1) * halo]

        @pl.when(p < count_rows - 1)
        def _(v=v):
            halo_copy(v, 1).start()

        @pl.when(p > 0)
        def _(v=v):
            halo_copy(v, 0).start()

    @pl.loop(0, off_count)
    def _(b):
        near[b] = jnp.dot(ext[:, :cells], hot_own[b], preferred_element_type=F32).astype(BF16)

    for v in range(var_count):
        total = jnp.zeros((panel, cells), F32)
        for w in range(var_count):
            total = total + (
                jself_ref[v, w:w + 1, :].astype(F32) * ext[w * panel:(w + 1) * panel, :cells].astype(F32)
            )
        acc[v] = total

    @pl.when(p > 0)
    def _():
        for v in range(var_count):
            halo_copy(v, 1).wait_recv()

    @pl.when(p < count_rows - 1)
    def _():
        for v in range(var_count):
            halo_copy(v, 0).wait_recv()

    width = 256 if cells % 256 == 0 else 128

    @pl.loop(0, cells // width)
    def _(tile):
        lanes = pl.ds(pl.multiple_of(tile * width, width), width)
        for b in range(off_count):
            far = jnp.dot(ext[:, cells:], hot_ghost[b, :, lanes], preferred_element_type=F32)
            both = far + near[b, :, lanes].astype(F32)
            for v in range(var_count):
                total = acc[v, :, lanes]
                for w in range(var_count):
                    total = total + (
                        joff_ref[v, w, b:b + 1, lanes].astype(F32) * both[w * panel:(w + 1) * panel]
                    )
                acc[v, :, lanes] = total

    for v in range(var_count):
        test = jnp.where(live, acc[v], 0.0).astype(BF16)
        test_ref[v] = test
        part = lax.dot_general(
            snap[v], test, (((1,), (1,)), ((), ())), preferred_element_type=F32
        )
        if v == 0:
            prod[...] = part
        else:
            prod[...] += part

    for k in range(1, count_modes):
        fan_copy(k, lax.rem(j + count_modes - k, count_modes)).wait_recv()

    high = prod[...].astype(BF16)
    low = (prod[...] - high.astype(F32)).astype(BF16)
    partial = jnp.dot(full[...], high, preferred_element_type=F32) + jnp.dot(
        full[...], low, preferred_element_type=F32
    )
    for d in range(count_rows):
        top = partial[d * rows_out:d * rows_out + half]
        bottom = partial[d * rows_out + half:(d + 1) * rows_out]
        out_box[d] = jnp.concatenate([top, bottom], axis=1)

    def red_copy(k):
        return pltpu.make_async_remote_copy(
            src_ref=out_box.at[row_peer(k)], dst_ref=in_box.at[k - 1], send_sem=red_send.at[k - 1],
            recv_sem=red_recv.at[k - 1], device_id=(row_peer(k), j), device_id_type=MESH,
        )

    for k in range(1, count_rows):
        red_copy(k).start()

    scales = 1.0 / jnp.sqrt(eigval_ref[...])
    mode_count = scales.shape[1]
    first = lax.broadcasted_iota(jnp.int32, (rows_out, mode_count), 0) + p * rows_out
    lane = lax.broadcasted_iota(jnp.int32, (rows_out, mode_count), 1)
    row_scales = jnp.sum(jnp.where(lane == first, scales, 0.0), axis=1, keepdims=True)
    col_scales = jnp.zeros((1, panel), F32)
    for other in range(count_modes):
        col_scales = col_scales + jnp.where(
            j == other, scales[:, other * panel:(other + 1) * panel], 0.0
        )

    for k in range(1, count_rows):
        ev_copy(k, p).wait_send()
    for k in range(1, count_modes):
        fan_copy(k, j).wait_send()

    @pl.when(p < count_rows - 1)
    def _():
        for v in range(var_count):
            halo_copy(v, 1).wait_send()

    @pl.when(p > 0)
    def _():
        for v in range(var_count):
            halo_copy(v, 0).wait_send()

    total = out_box[p]
    for k in range(1, count_rows):
        red_copy(k).wait_recv()
        total = total + in_box[k - 1]
    together = jnp.concatenate([total[:, :panel], total[:, panel:]], axis=0)
    red_ref[...] = together * row_scales * col_scales
    for k in range(1, count_rows):
        red_copy(k).wait_send()


def fused_shards(mesh, snapshots, eigvec, eigval, jac_self, jac_off, neighbor, send_list, send_count, owned_cells):
    count_rows, count_modes = mesh.shape["rows"], mesh.shape["modes"]
    snap_count, var_count, cells = snapshots.shape
    depth, panel = eigvec.shape
    off_count = neighbor.shape[0]
    halo = send_list.shape[1]
    modes = panel * count_modes
    rows_out = modes // count_rows
    whole = pl.BlockSpec(memory_space=pltpu.VMEM)
    scalars = pl.BlockSpec(memory_space=pltpu.SMEM)
    dma = pltpu.SemaphoreType.DMA
    flops = 2 * snap_count * panel * var_count * cells * 2 + 2 * panel * var_count * off_count * cells * (cells + 2 * halo)
    test, reduced = pl.pallas_call(
        functools.partial(kernel, count_rows, count_modes),
        out_shape=(
            jax.ShapeDtypeStruct((var_count, panel, cells), BF16),
            jax.ShapeDtypeStruct((rows_out, panel), F32),
        ),
        in_specs=[pl.BlockSpec(memory_space=pl.ANY)] + [whole] * 6 + [scalars] * 2,
        out_specs=(whole, whole),
        scratch_shapes=[
            pltpu.VMEM((var_count, snap_count, cells), BF16),
            pltpu.VMEM((modes, snap_count), BF16),
            pltpu.VMEM((var_count * panel, cells + 2 * halo), BF16),
            pltpu.VMEM((2, var_count * panel, halo), BF16),
            pltpu.VMEM((cells, 2 * halo), BF16),
            pltpu.VMEM((off_count, cells, cells), BF16),
            pltpu.VMEM((off_count, 2 * halo, cells), BF16),
            pltpu.VMEM((off_count, var_count * panel, cells), BF16),
            pltpu.VMEM((var_count, panel, cells), F32),
            pltpu.VMEM((snap_count, panel), F32),
            pltpu.VMEM((count_rows, rows_out // 2, 2 * panel), F32),
            pltpu.VMEM((count_rows - 1, rows_out // 2, 2 * panel), F32),
            dma((var_count,)),
            dma((count_rows - 1,)),
            dma((count_rows - 1,)),
            dma((count_modes - 1,)),
            dma((count_modes - 1,)),
            dma((2, var_count)),
            dma((2, var_count)),
            dma((count_rows - 1,)),
            dma((count_rows - 1,)),
        ],
        compiler_params=pltpu.CompilerParams(
            collective_id=0, has_side_effects=True, vmem_limit_bytes=48 * 1024 * 1024
        ),
        cost_estimate=pl.CostEstimate(
            flops=flops, bytes_accessed=2 * snap_count * var_count * cells, transcendentals=0
        ),
        name="galerkin",
    )(
        snapshots.transpose(1, 0, 2), eigvec.T, eigval.reshape(1, modes), jac_self,
        jac_off.transpose(1, 2, 0, 3), neighbor, send_list, send_count, owned_cells,
    )
    return test.transpose(1, 0, 2), reduced


def passed_along(value, axis, steps):
    count = lax.axis_size(axis)
    first, last = (max(0, -steps), min(count, count - steps))
    return lax.ppermute(value, axis, [(source, source + steps) for source in range(first, last)])


def take_slots(values, picks):
    chosen = (jnp.arange(values.shape[-1], dtype=jnp.int32)[:, None] == picks[None, :]).astype(BF16)
    return lax.dot_general(
        values, chosen, (((values.ndim - 1,), (0,)), ((), ())), preferred_element_type=F32
    ).astype(BF16)


def plain_shards(snapshots, eigvec, eigval, jac_self, jac_off, neighbor, send_list, send_count, owned_cells):
    snap_count, var_count, cell_count = snapshots.shape
    panel_width = eigvec.shape[1]
    halo_slots = send_list.shape[1]
    snap_rows = snapshots.reshape(snap_count, var_count * cell_count)
    modes_sum = lax.dot_general(
        lax.all_gather(eigvec, "rows", axis=0, tiled=True), snap_rows, (((0,), (0,)), ((), ())),
        preferred_element_type=F32,
    )
    owned_mask = jnp.arange(cell_count, dtype=jnp.int32)[None, None, :] < owned_cells[0]
    modes = jnp.where(
        owned_mask, modes_sum.reshape(panel_width, var_count, cell_count), jnp.zeros((), F32)
    ).astype(BF16)
    picked = take_slots(modes, send_list.reshape(-1)).reshape(panel_width, var_count, 2, halo_slots)
    live_slots = jnp.arange(halo_slots, dtype=jnp.int32)[None, :] < send_count
    picked = jnp.where(live_slots[None, None], picked, jnp.zeros((), BF16))
    from_below = passed_along(picked[:, :, 1], "rows", 1)
    from_above = passed_along(picked[:, :, 0], "rows", -1)
    extended = jnp.concatenate([modes, from_below, from_above], axis=2)
    total = jnp.einsum("vwc,mwc->mvc", jac_self, modes, preferred_element_type=F32)
    for b in range(neighbor.shape[0]):
        near = take_slots(extended, neighbor[b])
        total = total + jnp.einsum("vwc,mwc->mvc", jac_off[b], near, preferred_element_type=F32)
    test_local = jnp.where(owned_mask, total, jnp.zeros((), F32)).astype(BF16)
    products = lax.dot_general(
        snap_rows, test_local.reshape(panel_width, var_count * cell_count), (((1,), (1,)), ((), ())),
        preferred_element_type=F32,
    )
    shares = lax.psum_scatter(products, "rows", scatter_dimension=0, tiled=True)
    eigvec_rows = lax.all_gather(eigvec, "modes", axis=1, tiled=True)
    partial_sum = jnp.dot(eigvec_rows.astype(F32).T, shares, precision=lax.Precision.HIGHEST)
    reduced_part = lax.psum_scatter(partial_sum, "rows", scatter_dimension=0, tiled=True)
    rows_out = reduced_part.shape[0]
    scales = 1.0 / jnp.sqrt(eigval)
    row_scales = lax.dynamic_slice_in_dim(scales, lax.axis_index("rows") * rows_out, rows_out, 0)
    col_scales = lax.dynamic_slice_in_dim(scales, lax.axis_index("modes") * panel_width, panel_width, 0)
    return (test_local, reduced_part * row_scales[:, None] * col_scales[None, :])


def solution(mesh):
    in_specs = (
        P(None, None, "rows"),
        P("rows", "modes"),
        P(),
        P(None, None, "rows"),
        P(None, None, None, "rows"),
        P(None, "rows"),
        P(None, "rows"),
        P(None, "rows"),
        P("rows"),
    )
    out_specs = (P("modes", None, "rows"), P("rows", "modes"))

    def shards(*operands):
        snapshots, eigvec = operands[:2]
        send_list = operands[6]
        depth, panel = eigvec.shape
        rows_out = panel * mesh.shape["modes"] // mesh.shape["rows"]
        fits = (
            depth % 128 == 0 and panel == 64 and rows_out % 16 == 0
            and snapshots.shape[2] % 128 == 0 and send_list.shape[1] % 128 == 0
        )
        return fused_shards(mesh, *operands) if fits else plain_shards(*operands)

    return jax.shard_map(shards, mesh=mesh, in_specs=in_specs, out_specs=out_specs, check_vma=False)
```

time: 274 us -> 39.1 us (0.14)
  waiting for transfers between devices: 119 us -> 0 us
  local copies, waits for them, and re-layouts: 67.1 us -> 6.73 us
  blocking collectives: 33.1 us -> 0 us
  Pallas kernels: 0 us -> 30.7 us
  matrix products: 27.9 us -> 0 us
  between operations: 14.9 us -> 1.29 us
  other arithmetic: 5.69 us -> 0 us
  starting transfers between devices: 4.97 us -> 0 us
    unnamed x3 -> x0, waiting for transfers between devices: 61.3 us -> none
    reduce_scatter x1 -> x0, waiting for transfers between devices: 57.5 us -> none  [shards(): shares = lax.psum_scatter(products, 'rows', scatter_dimension=0, tiled=True)]
    all_gather x2 -> x0, blocking collectives: 33.1 us -> none  [the longest x1 27.9 us: shards(): lax.all_gather(eigvec, 'rows', axis=0, tiled=True)]
    pallas_call x0 -> x1, Pallas kernels: none -> 30.7 us  [fused_shards(): pl.pallas_call(functools.partial(kernel, count_rows, count_modes), out_sh...]
    dot_general x5 -> x0, matrix products: 27.9 us -> none  [the longest x1 9.62 us: shards(): jnp.einsum('bvwc,mwbc->mvc', jac_off, neighbours, preferred_element_type=...]
    gather x4 -> x0, local copies, waits for them, and re-layouts: 25 us -> none  [the longest x2 22.8 us: shards(): neighbours = jnp.take(extended, neighbor, axis=2)]
    unnamed x24 -> x15, local copies, waits for them, and re-layouts: 23.4 us -> 6.73 us
    select_n x1 -> x0, local copies, waits for them, and re-layouts: 14.5 us -> none  [shards(): neighbours = jnp.take(extended, neighbor, axis=2)]
  transfers between devices with their start and end apart: 4 -> 0, of which waited for: 2 -> 0; matrix products, arithmetic and copies ran while one was open for 3% -> 0% of each run, Pallas kernels for 0% -> 0%
where the time goes in v1:
time: 39.1 us; the launch traced here: 38.8 us
  Pallas kernels  30.7 us (79%)
  local copies, waits for them, and re-layouts  6.73 us (17%)
  between operations  1.29 us (3%)
    pallas_call x1, Pallas kernels, fused_shards(): pl.pallas_call(functools.partial(kernel, count_rows, count_modes), out_sh...  30.7 us
    unnamed x15, local copies, waits for them, and re-layouts  6.73 us

profile of v1, /device:TPU:0, one launch (start us, length us, event | category | flops | bytes accessed | tf_op | source)
XLA Modules:
  0.0 38.8 jit_solution(14138667378276102798)
XLA Ops:
  1.3 0.7 %copy.11.scount_ref = s32[2,1]{1,0:T(2,128)S(1)} copy(s32[2,1]{0,1:T(1,128)} %param.16) | data formatting | bytes 16 | tf_op args[7]
  2.0 0.0 copy-start
  2.0 1.0 %copy-done = bf16[6,5,5,768]{3,0,2,1:T(8,128)(2,1)S(1)} copy-done((bf16[6,5,5,768]{3,0,2,1:T(8,128)(2,1)S(1)}, bf16[6,5,5,768]{3,0,2,1:T(8,128)(2,1)}, u32[]{:S(2)}) %copy-start) | copy-done | bytes 230424
  3.0 0.0 copy-start.1
  3.0 0.8 %copy-done.1 = bf16[5,5,768]{2,1,0:T(8,128)(2,1)S(1)} copy-done((bf16[5,5,768]{2,1,0:T(8,128)(2,1)S(1)}, bf16[5,5,768]{2,1,0:T(8,128)(2,1)}, u32[]{:S(2)}) %copy-start.1) | copy-done | bytes 38424
  3.8 0.0 copy-start.2
  3.8 0.7 %copy-done.2 = s32[6,768]{1,0:T(8,128)S(1)} copy-done((s32[6,768]{1,0:T(8,128)S(1)}, s32[6,768]{1,0:T(8,128)}, u32[]{:S(2)}) %copy-start.2) | copy-done | bytes 18456
  4.6 0.0 copy-start.3
  4.6 0.7 %copy-done.3 = bf16[128,64]{0,1:T(8,128)(2,1)S(1)} copy-done((bf16[128,64]{0,1:T(8,128)(2,1)S(1)}, bf16[128,64]{0,1:T(8,128)(2,1)}, u32[]{:S(2)}) %copy-start.3) | copy-done | bytes 16408
  5.3 0.0 copy-start.4
  5.3 0.7 %copy-done.4 = s32[2,256]{1,0:T(2,128)S(1)} copy-done((s32[2,256]{1,0:T(2,128)S(1)}, s32[2,256]{1,0:T(2,128)}, u32[]{:S(2)}) %copy-start.4) | copy-done | bytes 2072
  6.0 0.0 copy-start.5
  6.0 0.7 %copy-done.5 = f32[256]{0:T(256)S(1)} copy-done((f32[256]{0:T(256)S(1)}, f32[256]{0:T(256)}, u32[]{:S(2)}) %copy-start.5) | copy-done | bytes 1048
  6.6 30.7 %galerkin.1 = (bf16[5,64,768]{2,1,0:T(8,128)(2,1)S(1)}, f32[32,64]{1,0:T(8,128)S(1)}) custom-call(bf16[5,1024,768]{2,1,0:T(8,128)(2,1)} %bitcast.9, bf16[64,128]{1,0:T(8,128)(2,1)S(1)} %bitcast.7, f32[1,256]{1,0:T(1,128)S(1)} %bitcast.8, bf16[5,5,768]{2,1,0:T(8,128)(2,1)S(1)} %copy-done.1, bf16[5,5,6,768]{3,2,1,0:T(8,128)(2,1)S(1)} %bitcast.6, ...), custom_call_target="tpu_custom_call" | custom-call | flops 4781506560 | bytes 7864320 | tf_op jit(solution)/shard_map/galerkin/pallas_call | solution.py:255
  37.4 0.8 %copy.15 = bf16[64,5,768]{2,0,1:T(8,128)(2,1)} copy(bf16[64,5,768]{2,0,1:T(8,128)(2,1)S(1)} %bitcast.5) | data formatting | bytes 983040
  38.2 0.6 %copy.16 = f32[32,64]{1,0:T(8,128)} copy(f32[32,64]{1,0:T(8,128)S(1)} %get-tuple-element.9) | data formatting | bytes 16384
Async XLA Ops:
  2.0 1.0 %copy-start = (bf16[6,5,5,768]{3,0,2,1:T(8,128)(2,1)S(1)}, bf16[6,5,5,768]{3,0,2,1:T(8,128)(2,1)}, u32[]{:S(2)}) copy-start(bf16[6,5,5,768]{3,0,2,1:T(8,128)(2,1)} %param.13) | copy-start | bytes 691204
  3.0 0.8 %copy-start.1 = (bf16[5,5,768]{2,1,0:T(8,128)(2,1)S(1)}, bf16[5,5,768]{2,1,0:T(8,128)(2,1)}, u32[]{:S(2)}) copy-start(bf16[5,5,768]{2,1,0:T(8,128)(2,1)} %jself_ref.1) | copy-start | bytes 115204
  3.8 0.7 %copy-start.2 = (s32[6,768]{1,0:T(8,128)S(1)}, s32[6,768]{1,0:T(8,128)}, u32[]{:S(2)}) copy-start(s32[6,768]{1,0:T(8,128)} %nbr_ref.1) | copy-start | bytes 55300
  4.6 0.7 %copy-start.3 = (bf16[128,64]{0,1:T(8,128)(2,1)S(1)}, bf16[128,64]{0,1:T(8,128)(2,1)}, u32[]{:S(2)}) copy-start(bf16[128,64]{0,1:T(8,128)(2,1)} %param.10) | copy-start | bytes 49156
  5.3 0.7 %copy-start.4 = (s32[2,256]{1,0:T(2,128)S(1)}, s32[2,256]{1,0:T(2,128)}, u32[]{:S(2)}) copy-start(s32[2,256]{1,0:T(2,128)} %slist_ref.1) | copy-start | bytes 6148
  6.0 0.7 %copy-start.5 = (f32[256]{0:T(256)S(1)}, f32[256]{0:T(256)}, u32[]{:S(2)}) copy-start(f32[256]{0:T(256)} %param.11) | copy-start | bytes 3076

commit v2 on v1

--- a/solution.py
+++ b/solution.py
@@ -19,20 +19,32 @@
 
 def kernel(
     count_rows, count_modes,
-    snap_hbm, ev_ref, eigval_ref, jself_ref, joff_ref, nbr_ref, slist_ref, scount_ref, owned_ref,
-    test_ref, red_ref,
-    snap, full, ext, pack, hot_send, hot_own, hot_ghost, near, acc, prod, out_box, in_box,
-    snap_sem, ev_send, ev_recv, fan_send, fan_recv, halo_send, halo_recv, red_send, red_recv,
+    snap_hbm, ev_hbm, eigval_hbm, jself_hbm, joff_hbm, nbr_hbm, slist_hbm, scount_hbm, owned_hbm,
+    test_hbm, red_ref,
+    test_ref, eigval_ref, jself_ref, joff_ref, nbr_ref, slist_ref, scount_ref, owned_ref, snap, full, ext, pack, hot_send, hot_own, hot_ghost, near, acc, prod, out_box, in_box,
+    load_sem, test_sem, snap_sem, ev_send, ev_recv, fan_send, fan_recv, halo_send, halo_recv, red_send, red_recv,
 ):
     p = lax.axis_index("rows")
     j = lax.axis_index("modes")
     var_count, snap_count, cells = snap.shape
-    panel, depth = ev_ref.shape
+    panel, depth = ev_hbm.shape
     off_count = nbr_ref.shape[0]
     halo = slist_ref.shape[1]
     rows_out = red_ref.shape[0]
     half = rows_out // 2
 
+    mine_slice = full.at[
+        pl.ds(pl.multiple_of(j * panel, panel), panel), pl.ds(pl.multiple_of(p * depth, depth), depth)
+    ]
+    loads = [
+        pltpu.make_async_copy(source, target, load_sem.at[i])
+        for i, (source, target) in enumerate((
+            (nbr_hbm, nbr_ref), (slist_hbm, slist_ref), (scount_hbm, scount_ref), (owned_hbm, owned_ref),
+            (ev_hbm, mine_slice), (jself_hbm, jself_ref), (joff_hbm, joff_ref), (eigval_hbm, eigval_ref),
+        ))
+    ]
+    for copy in loads:
+        copy.start()
     snap_copies = [
         pltpu.make_async_copy(snap_hbm.at[v], snap.at[v], snap_sem.at[v]) for v in range(var_count)
     ]
@@ -60,20 +72,18 @@
 
     def ev_copy(k, source):
         return pltpu.make_async_remote_copy(
-            src_ref=ev_ref, dst_ref=panel_slice(j, source), send_sem=ev_send.at[k - 1],
+            src_ref=ev_hbm, dst_ref=panel_slice(j, source), send_sem=ev_send.at[k - 1],
             recv_sem=ev_recv.at[k - 1], device_id=(row_peer(k), j), device_id_type=MESH,
         )
 
     for k in range(1, count_rows):
         ev_copy(k, p).start()
 
-    full[
-        pl.ds(pl.multiple_of(j * panel, panel), panel), pl.ds(pl.multiple_of(p * depth, depth), depth)
-    ] = ev_ref[...]
-
+    for copy in loads:
+        copy.wait()
     slot = lax.broadcasted_iota(jnp.int32, (1, halo), 1)
     for way in range(2):
-        picks = jnp.where(slot < scount_ref[way, 0], slist_ref[pl.ds(way, 1), :], -1)
+        picks = jnp.where(slot < scount_ref[0, way], slist_ref[pl.ds(way, 1), :], -1)
         hot_send[:, way * halo:(way + 1) * halo] = one_hot(picks, 0, cells)
 
     @pl.loop(0, off_count)
@@ -145,35 +155,40 @@
             )
         acc[v] = total
 
-    @pl.when(p > 0)
-    def _():
-        for v in range(var_count):
-            halo_copy(v, 1).wait_recv()
-
-    @pl.when(p < count_rows - 1)
-    def _():
-        for v in range(var_count):
-            halo_copy(v, 0).wait_recv()
-
     width = 256 if cells % 256 == 0 else 128
 
-    @pl.loop(0, cells // width)
-    def _(tile):
-        lanes = pl.ds(pl.multiple_of(tile * width, width), width)
-        for b in range(off_count):
-            far = jnp.dot(ext[:, cells:], hot_ghost[b, :, lanes], preferred_element_type=F32)
-            both = far + near[b, :, lanes].astype(F32)
-            for v in range(var_count):
-                total = acc[v, :, lanes]
-                for w in range(var_count):
-                    total = total + (
-                        joff_ref[v, w, b:b + 1, lanes].astype(F32) * both[w * panel:(w + 1) * panel]
-                    )
-                acc[v, :, lanes] = total
+    lots = (range(0, 2), range(2, var_count))
+    for lot in lots:
+        @pl.when(p > 0)
+        def _(lot=lot):
+            for v in lot:
+                halo_copy(v, 1).wait_recv()
+
+        @pl.when(p < count_rows - 1)
+        def _(lot=lot):
+            for v in lot:
+                halo_copy(v, 0).wait_recv()
+
+        rows = slice(lot[0] * panel, (lot[-1] + 1) * panel)
+
+        @pl.loop(0, cells // width)
+        def _(tile, lot=lot, rows=rows):
+            lanes = pl.ds(pl.multiple_of(tile * width, width), width)
+            for b in range(off_count):
+                far = jnp.dot(ext[rows, cells:], hot_ghost[b, :, lanes], preferred_element_type=F32)
+                both = far + near[b, rows, lanes].astype(F32)
+                for v in range(var_count):
+                    total = acc[v, :, lanes]
+                    for i, w in enumerate(lot):
+                        total = total + (
+                            joff_ref[v, w, b:b + 1, lanes].astype(F32) * both[i * panel:(i + 1) * panel]
+                        )
+                    acc[v, :, lanes] = total
 
     for v in range(var_count):
         test = jnp.where(live, acc[v], 0.0).astype(BF16)
         test_ref[v] = test
+        pltpu.make_async_copy(test_ref.at[v], test_hbm.at[v], test_sem.at[v]).start()
         part = lax.dot_general(
             snap[v], test, (((1,), (1,)), ((), ())), preferred_element_type=F32
         )
@@ -230,6 +245,9 @@
         for v in range(var_count):
             halo_copy(v, 0).wait_send()
 
+    for v in range(var_count):
+        pltpu.make_async_copy(test_ref.at[v], test_hbm.at[v], test_sem.at[v]).wait()
+
     total = out_box[p]
     for k in range(1, count_rows):
         red_copy(k).wait_recv()
@@ -249,7 +267,6 @@
     modes = panel * count_modes
     rows_out = modes // count_rows
     whole = pl.BlockSpec(memory_space=pltpu.VMEM)
-    scalars = pl.BlockSpec(memory_space=pltpu.SMEM)
     dma = pltpu.SemaphoreType.DMA
     flops = 2 * snap_count * panel * var_count * cells * 2 + 2 * panel * var_count * off_count * cells * (cells + 2 * halo)
     test, reduced = pl.pallas_call(
@@ -258,9 +275,17 @@
             jax.ShapeDtypeStruct((var_count, panel, cells), BF16),
             jax.ShapeDtypeStruct((rows_out, panel), F32),
         ),
-        in_specs=[pl.BlockSpec(memory_space=pl.ANY)] + [whole] * 6 + [scalars] * 2,
-        out_specs=(whole, whole),
+        in_specs=[pl.BlockSpec(memory_space=pl.ANY)] * 9,
+        out_specs=(pl.BlockSpec(memory_space=pl.ANY), whole),
         scratch_shapes=[
+            pltpu.VMEM((var_count, panel, cells), BF16),
+            pltpu.VMEM((1, modes), F32),
+            pltpu.VMEM(jac_self.shape, BF16),
+            pltpu.VMEM((var_count, var_count, off_count, cells), BF16),
+            pltpu.VMEM(neighbor.shape, jnp.int32),
+            pltpu.VMEM(send_list.shape, jnp.int32),
+            pltpu.SMEM((1, 2), jnp.int32),
+            pltpu.SMEM((1,), jnp.int32),
             pltpu.VMEM((var_count, snap_count, cells), BF16),
             pltpu.VMEM((modes, snap_count), BF16),
             pltpu.VMEM((var_count * panel, cells + 2 * halo), BF16),
@@ -273,6 +298,8 @@
             pltpu.VMEM((snap_count, panel), F32),
             pltpu.VMEM((count_rows, rows_out // 2, 2 * panel), F32),
             pltpu.VMEM((count_rows - 1, rows_out // 2, 2 * panel), F32),
+            dma((8,)),
+            dma((var_count,)),
             dma((var_count,)),
             dma((count_rows - 1,)),
             dma((count_rows - 1,)),
@@ -284,7 +311,7 @@
             dma((count_rows - 1,)),
         ],
         compiler_params=pltpu.CompilerParams(
-            collective_id=0, has_side_effects=True, vmem_limit_bytes=48 * 1024 * 1024
+            collective_id=0, has_side_effects=True, vmem_limit_bytes=58 * 1024 * 1024
         ),
         cost_estimate=pl.CostEstimate(
             flops=flops, bytes_accessed=2 * snap_count * var_count * cells, transcendentals=0
@@ -292,7 +319,7 @@
         name="galerkin",
     )(
         snapshots.transpose(1, 0, 2), eigvec.T, eigval.reshape(1, modes), jac_self,
-        jac_off.transpose(1, 2, 0, 3), neighbor, send_list, send_count, owned_cells,
+        jac_off.transpose(1, 2, 0, 3), neighbor, send_list, send_count.T, owned_cells,
     )
     return test.transpose(1, 0, 2), reduced
 

time: 39.1 us -> 35.7 us (0.913)
  local copies, waits for them, and re-layouts: 6.73 us -> 3.16 us
    unnamed x15 -> x2, local copies, waits for them, and re-layouts: 6.73 us -> 3.16 us
where the time goes in v2:
time: 35.7 us; the launch traced here: 35.5 us
  Pallas kernels  31 us (87%)
  local copies, waits for them, and re-layouts  3.16 us (9%)
  between operations  1.29 us (4%)
    pallas_call x1, Pallas kernels, fused_shards(): pl.pallas_call(functools.partial(kernel, count_rows, count_modes), out_sh...  31 us
    unnamed x2, local copies, waits for them, and re-layouts  3.16 us

profile of v2, /device:TPU:0, one launch (start us, length us, event | category | flops | bytes accessed | tf_op | source)
XLA Modules:
  0.0 35.5 jit_solution(7682812301970086640)
XLA Ops:
  1.3 31.0 %galerkin.1 = (bf16[5,64,768]{2,1,0:T(8,128)(2,1)}, f32[32,64]{1,0:T(8,128)}) custom-call(bf16[5,1024,768]{2,1,0:T(8,128)(2,1)} %bitcast.7, bf16[64,128]{1,0:T(8,128)(2,1)} %bitcast.9, f32[1,256]{1,0:T(1,128)} %bitcast.10, bf16[5,5,768]{2,1,0:T(8,128)(2,1)} %jself_hbm.1, bf16[5,5,6,768]{3,2,1,0:T(8,128)(2,1)} %bitcast.8, s32[6,768]{1,0:T(8,128)} %nbr_hbm.1, ...), custom_call_target="tpu_custom_call" | custom-call | flops 4781506560 | bytes 7864320 | tf_op jit(solution)/shard_map/galerkin/pallas_call | solution.py:272
  32.3 1.8 %copy.14 = bf16[64,5,768]{2,0,1:T(8,128)(2,1)} copy(bf16[64,5,768]{2,0,1:T(8,128)(2,1)} %bitcast.6) | data formatting | bytes 983040
  34.2 1.3 %copy.15 = f32[32,64]{1,0:T(8,128)} copy(f32[32,64]{1,0:T(8,128)} %get-tuple-element.9) | data formatting | bytes 16384

commit v3 on v2

--- a/solution.py
+++ b/solution.py
@@ -21,7 +21,7 @@
     count_rows, count_modes,
     snap_hbm, ev_hbm, eigval_hbm, jself_hbm, joff_hbm, nbr_hbm, slist_hbm, scount_hbm, owned_hbm,
     test_hbm, red_ref,
-    test_ref, eigval_ref, jself_ref, joff_ref, nbr_ref, slist_ref, scount_ref, owned_ref, snap, full, ext, pack, hot_send, hot_own, hot_ghost, near, acc, prod, out_box, in_box,
+    test_ref, eigval_ref, jself_ref, joff_ref, nbr_ref, slist_ref, scount_ref, owned_ref, snap, full, ext, pack, hot_send, hot_own, hot_ghost, near, acc, out_box, in_box,
     load_sem, test_sem, snap_sem, ev_send, ev_recv, fan_send, fan_recv, halo_send, halo_recv, red_send, red_recv,
 ):
     p = lax.axis_index("rows")
@@ -126,22 +126,26 @@
         )
 
     mine = full[pl.ds(pl.multiple_of(j * panel, panel), panel), :]
-    for v in range(var_count):
-        snap_copies[v].wait()
-        own = jnp.dot(mine, snap[v], preferred_element_type=F32)
-        own = jnp.where(live, own, 0.0).astype(BF16)
-        ext[v * panel:(v + 1) * panel, :cells] = own
-        sent = jnp.dot(own, hot_send[...], preferred_element_type=F32).astype(BF16)
+    lots = (range(0, 2), range(2, var_count))
+    for lot in lots:
+        for v in lot:
+            snap_copies[v].wait()
+            own = jnp.dot(mine, snap[v], preferred_element_type=F32)
+            ext[v * panel:(v + 1) * panel, :cells] = jnp.where(live, own, 0.0).astype(BF16)
+        rows = slice(lot[0] * panel, (lot[-1] + 1) * panel)
+        sent = jnp.dot(ext[rows, :cells], hot_send[...], preferred_element_type=F32).astype(BF16)
         for way in range(2):
-            pack[way, v * panel:(v + 1) * panel, :] = sent[:, way * halo:(way + 1) * halo]
+            pack[way, rows, :] = sent[:, way * halo:(way + 1) * halo]
 
         @pl.when(p < count_rows - 1)
-        def _(v=v):
-            halo_copy(v, 1).start()
+        def _(lot=lot):
+            for v in lot:
+                halo_copy(v, 1).start()
 
         @pl.when(p > 0)
-        def _(v=v):
-            halo_copy(v, 0).start()
+        def _(lot=lot):
+            for v in lot:
+                halo_copy(v, 0).start()
 
     @pl.loop(0, off_count)
     def _(b):
@@ -157,7 +161,6 @@
 
     width = 256 if cells % 256 == 0 else 128
 
-    lots = (range(0, 2), range(2, var_count))
     for lot in lots:
         @pl.when(p > 0)
         def _(lot=lot):
@@ -192,19 +195,17 @@
         part = lax.dot_general(
             snap[v], test, (((1,), (1,)), ((), ())), preferred_element_type=F32
         )
-        if v == 0:
-            prod[...] = part
-        else:
-            prod[...] += part
+        products = part if v == 0 else products + part
 
     for k in range(1, count_modes):
         fan_copy(k, lax.rem(j + count_modes - k, count_modes)).wait_recv()
 
-    high = prod[...].astype(BF16)
-    low = (prod[...] - high.astype(F32)).astype(BF16)
-    partial = jnp.dot(full[...], high, preferred_element_type=F32) + jnp.dot(
-        full[...], low, preferred_element_type=F32
+    high = products.astype(BF16)
+    low = (products - high.astype(F32)).astype(BF16)
+    split = jnp.dot(
+        full[...], jnp.concatenate([high, low], axis=1), preferred_element_type=F32
     )
+    partial = split[:, :panel] + split[:, panel:]
     for d in range(count_rows):
         top = partial[d * rows_out:d * rows_out + half]
         bottom = partial[d * rows_out + half:(d + 1) * rows_out]
@@ -295,7 +296,6 @@
             pltpu.VMEM((off_count, 2 * halo, cells), BF16),
             pltpu.VMEM((off_count, var_count * panel, cells), BF16),
             pltpu.VMEM((var_count, panel, cells), F32),
-            pltpu.VMEM((snap_count, panel), F32),
             pltpu.VMEM((count_rows, rows_out // 2, 2 * panel), F32),
             pltpu.VMEM((count_rows - 1, rows_out // 2, 2 * panel), F32),
             dma((8,)),

time: 35.7 us -> 35.4 us (level)
  no operation moved by 1% of the time
where the time goes in v3:
time: 35.4 us; the launch traced here: 35.2 us
  Pallas kernels  30.7 us (87%)
  local copies, waits for them, and re-layouts  3.16 us (9%)
  between operations  1.29 us (4%)
    pallas_call x1, Pallas kernels, fused_shards(): pl.pallas_call(functools.partial(kernel, count_rows, count_modes), out_sh...  30.7 us
    unnamed x2, local copies, waits for them, and re-layouts  3.16 us

profile of v3, /device:TPU:0, one launch (start us, length us, event | category | flops | bytes accessed | tf_op | source)
XLA Modules:
  0.0 35.2 jit_solution(695776712605194183)
XLA Ops:
  1.3 30.7 %galerkin.1 = (bf16[5,64,768]{2,1,0:T(8,128)(2,1)}, f32[32,64]{1,0:T(8,128)}) custom-call(bf16[5,1024,768]{2,1,0:T(8,128)(2,1)} %bitcast.7, bf16[64,128]{1,0:T(8,128)(2,1)} %bitcast.9, f32[1,256]{1,0:T(1,128)} %bitcast.10, bf16[5,5,768]{2,1,0:T(8,128)(2,1)} %jself_hbm.1, bf16[5,5,6,768]{3,2,1,0:T(8,128)(2,1)} %bitcast.8, s32[6,768]{1,0:T(8,128)} %nbr_hbm.1, ...), custom_call_target="tpu_custom_call" | custom-call | flops 4781506560 | bytes 7864320 | tf_op jit(solution)/shard_map/galerkin/pallas_call | solution.py:273
  32.0 1.8 %copy.14 = bf16[64,5,768]{2,0,1:T(8,128)(2,1)} copy(bf16[64,5,768]{2,0,1:T(8,128)(2,1)} %bitcast.6) | data formatting | bytes 983040
  33.8 1.3 %copy.15 = f32[32,64]{1,0:T(8,128)} copy(f32[32,64]{1,0:T(8,128)} %get-tuple-element.9) | data formatting | bytes 16384
